TPU v7x, 512 devices: a whole 4x4x16 slice. The times are simulated.
512 devices in a mesh: dp: 32 (over z_hi, x, core), tensor: 16 (over z_lo, y).
Axes of the slice: x: 4, y: 4, z: 16 (z_hi: 4, z_lo: 4; z = z_hi * 4 + z_lo), core: 2. Of those that a mesh axis runs over, the one named last changes fastest.
Arguments:
- queries: bfloat16 [4096, 4096], P('dp', 'tensor'), may hold values from -150 to 150
- keys: bfloat16 [4096, 1024], P('dp'), may hold values from -6 to 6
- values: bfloat16 [4096, 1024], P('dp'), may hold values from -6 to 6
- doc_start: int32 [4096], P('dp'), may hold values from 0 to 4094, as said below
- out_weight: bfloat16 [4096, 8192], P('tensor', 'dp'), may hold values from -0.09375 to 0.09375
- residual: bfloat16 [4096, 8192], P('dp', 'tensor'), may hold values from -60 to 60
- gain: bfloat16 [8192], P('tensor'), may hold values from 0.5 to 1.5
- cotangent: bfloat16 [4096, 8192], P('dp', 'tensor'), may hold values from -6 to 6
Outputs:
- mixed: bfloat16 [4096, 8192], P('dp', 'tensor')
- normed: bfloat16 [4096, 8192], P('dp', 'tensor')
- grad_weight: bfloat16 [4096, 8192], P('tensor', 'dp')
- grad_heads: bfloat16 [4096, 4096], P('dp', 'tensor')
Inputs may be any that keep to these rules, and one draw needn't show every extreme that they name: doc_start[i] <= i, doc_start[i] lies in the same block of 128 rows as i, and equals i or doc_start[i - 1]; the first row of each block starts a document.
All inputs are finite; a program needn't handle non-finite values.
Results may differ from a plain program's by a relative error of at most 0.024.
Values may be sent and summed in bfloat16 or wider, within the bound.
A program may use at most 64 MiB of HBM per device.

v0:
```python
import math

import jax
import jax.numpy as jnp
from jax import lax
from jax.sharding import PartitionSpec as P

HD = 128
KV_HEADS = 8
H_DEV = 2


def finish_rows(partial_value, resid_rows, gain, tensor_index):
    columns = resid_rows.shape[1]
    offset = tensor_index * columns
    local_cols = lax.dynamic_slice_in_dim(partial_value, offset, columns, 1) + resid_rows.astype(
        jnp.float32
    )
    placed = lax.dynamic_update_slice_in_dim(partial_value, local_cols, offset, 1)
    total = lax.psum(placed.astype(jnp.bfloat16), "tensor").astype(jnp.float32)
    mean_square = jnp.mean(total * total, axis=1)
    owned = lax.dynamic_slice_in_dim(total, offset, columns, 1)
    factor = lax.rsqrt(mean_square + 1e-05)[:, None]
    normed_rows = (owned * factor * gain.astype(jnp.float32)[None, :]).astype(jnp.bfloat16)
    return (owned.astype(jnp.bfloat16), normed_rows)


def body(queries, keys, values, doc_start, out_weight, residual, gain, cotangent):
    count = queries.shape[0]
    tensor_index = lax.axis_index("tensor")
    data_index = lax.axis_index("dp")
    group_size = H_DEV * lax.axis_size("tensor") // KV_HEADS
    position = jnp.arange(count, dtype=jnp.int32)
    starts = doc_start - data_index * count
    allowed = (position[None, :] >= starts[:, None]) & (position[None, :] <= position[:, None])
    results = []
    for head in range(H_DEV):
        kv_head = (tensor_index * H_DEV + head) // group_size
        key_rows = lax.dynamic_slice_in_dim(keys, kv_head * HD, HD, 1)
        value_rows = lax.dynamic_slice_in_dim(values, kv_head * HD, HD, 1)
        query_rows = queries[:, head * HD : (head + 1) * HD]
        scores = jnp.einsum(
            "id,jd->ij", query_rows, key_rows, preferred_element_type=jnp.float32
        ) / math.sqrt(HD)
        scores = jnp.where(allowed, scores, -1e30)
        top = jnp.max(scores, axis=-1, keepdims=True)
        weights = jnp.where(allowed, jnp.exp(scores - top), 0.0)
        probs = (weights / jnp.sum(weights, axis=-1, keepdims=True)).astype(jnp.bfloat16)
        results.append(
            jnp.dot(probs, value_rows, preferred_element_type=jnp.float32).astype(jnp.bfloat16)
        )
    heads_out = jnp.concatenate(results, axis=1)
    full_weight = lax.all_gather(out_weight, "dp", axis=1, tiled=True)
    partial_value = jnp.dot(heads_out, full_weight, preferred_element_type=jnp.float32)
    mixed_rows, normed_rows = finish_rows(partial_value, residual, gain, tensor_index)
    full_cot = lax.all_gather(cotangent, "tensor", axis=1, tiled=True)
    grad_heads = jnp.einsum(
        "id,kd->ik", full_cot, full_weight, preferred_element_type=jnp.float32
    ).astype(jnp.bfloat16)
    weight_term = jnp.einsum(
        "ik,id->kd", heads_out, full_cot, preferred_element_type=jnp.float32
    ).astype(jnp.bfloat16)
    grad_weight = (
        lax.psum_scatter(weight_term, "dp", scatter_dimension=1, tiled=True)
        .astype(jnp.float32)
        .astype(jnp.bfloat16)
    )
    return (mixed_rows, normed_rows, grad_weight, grad_heads)


def solution(mesh):
    placed = (
        P("dp", "tensor"),
        P("dp", None),
        P("dp", None),
        P("dp"),
        P("tensor", "dp"),
        P("dp", "tensor"),
        P("tensor"),
        P("dp", "tensor"),
    )
    return jax.shard_map(
        body,
        mesh=mesh,
        in_specs=placed,
        out_specs=(P("dp", "tensor"), P("dp", "tensor"), P("tensor", "dp"), P("dp", "tensor")),
        check_vma=False,
    )
```

profile of v0, /device:TPU:1, one launch (start us, length us, event | category | flops | bytes accessed | tf_op | source)
XLA Modules:
  0.0 532.2 jit_solution(1162548555076287512)
XLA Ops:
  7.2 0.0 copy-start
  7.2 0.0 all-gather.3.cloned.1.call-start
  7.2 0.7 all-gather.3.cloned.1.call-update
  7.9 0.0 all-gather.5.cloned.1.call-start
  8.0 0.7 all-gather.5.cloned.1.call-update
  8.7 0.0 all-reduce.2.cloned.1.call-start
  8.7 0.7 broadcast_subtract_fusion
  9.4 0.0 copy-done
  9.4 0.9 fusion.23
  10.3 0.9 fusion.22
  11.3 0.1 fusion.5
  11.3 1.0 convolution_convert_fusion.2
  12.3 1.0 convolution_convert_fusion.3
  13.3 0.0 copy-start.3
  13.3 107.1 %all-gather.3.cloned.1.call-done = bf16[256,8192]{1,0:T(8,128)(2,1)} async-done(((bf16[256,256]{1,0:T(8,128)(2,1)}), bf16[256,8192]{1,0:T(8,128)(2,1)}) %all-gather.3.cloned.1.call-update) | async-done | bytes 4194320 | tf_op jit(solution)/shard_map/all_gather | solution.py:53
  120.4 2.9 fusion.7
  123.3 0.0 copy-done.3
  123.4 1.6 convert_element_type.43
  125.0 0.0 all-reduce.2.cloned.1.call-update
  125.0 0.0 copy-start.4
  125.0 0.0 reduce-scatter.2.cloned.1.call-start
  125.0 70.3 %all-gather.5.cloned.1.call-done = bf16[128,8192]{1,0:T(8,128)(2,1)} async-done(((bf16[128,512]{1,0:T(8,128)(2,1)}), bf16[128,8192]{1,0:T(8,128)(2,1)}) %all-gather.5.cloned.1.call-update) | async-done | bytes 2097168 | tf_op jit(solution)/shard_map/all_gather | solution.py:56
  195.3 0.0 copy-start.1
  195.3 5.0 convolution_convert_fusion
  200.3 0.0 reduce-scatter.2.cloned.1.call-update
  200.3 0.0 copy-done.4
  200.3 0.0 copy-done.1
  200.3 4.4 convolution_convert_fusion.1
  204.7 169.7 %all-reduce.2.cloned.1.call-done = bf16[128,8192]{1,0:T(8,128)(2,1)} async-done(((bf16[128,8192]{1,0:T(8,128)(2,1)}), bf16[128,8192]{1,0:T(8,128)(2,1)}) %all-reduce.2.cloned.1.call-update) | async-done | bytes 2097168 | tf_op jit(solution)/shard_map/psum | solution.py:20
  374.4 0.0 copy-start.2
  374.4 2.1 convert_element_type.44
  376.6 0.7 dynamic-slice_convert_fusion
  377.2 0.0 copy-done.2
  377.2 0.5 multiply_reduce_fusion
  377.7 0.8 multiply_convert_fusion
  378.5 147.2 %reduce-scatter.2.cloned.1.call-done = bf16[256,256]{1,0:T(8,128)(2,1)} async-done(((bf16[256,8192]{1,0:T(8,128)(2,1)}), bf16[256,256]{1,0:T(8,128)(2,1)}) %reduce-scatter.2.cloned.1.call-update) | async-done | bytes 131088 | tf_op jit(solution)/shard_map/reduce_scatter | solution.py:64
  (3 shorter events, 0.1 us)
Async XLA Ops:
  7.2 2.2 copy-start
  7.2 113.2 %all-gather.3.cloned.1.call-start = ((), (), s32[]{:S(2)}) async-start(), calls=%async_computation.1 | async-start | bytes 4325376 | tf_op jit(solution)/shard_map/all_gather | solution.py:53
  7.9 187.4 %all-gather.5.cloned.1.call-start = ((), (), s32[]{:S(2)}) async-start(), calls=%async_computation.3 | async-start | bytes 2228224 | tf_op jit(solution)/shard_map/all_gather | solution.py:56
  8.7 365.7 %all-reduce.2.cloned.1.call-start = ((), (), s32[]{:S(2)}) async-start(), calls=%async_computation.2 | async-start | bytes 4194304 | tf_op jit(solution)/shard_map/psum | solution.py:20
  13.3 110.1 %copy-start.3 = (bf16[128,512]{1,0:T(8,128)(2,1)S(1)}, bf16[128,512]{1,0:T(8,128)(2,1)}, u32[]{:S(2)}) copy-start(bf16[128,512]{1,0:T(8,128)(2,1)} %param.13) | copy-start | bytes 393220
  125.0 75.3 %copy-start.4 = (bf16[512]{0:T(512)(128)(2,1)S(1)}, bf16[512]{0:T(512)(128)(2,1)}, u32[]{:S(2)}) copy-start(bf16[512]{0:T(512)(128)(2,1)} %param.14) | copy-start | bytes 3076
  125.0 400.7 %reduce-scatter.2.cloned.1.call-start = ((), (), s32[]{:S(2)}) async-start(), calls=%async_computation.4 | async-start | bytes 4325376 | tf_op jit(solution)/shard_map/reduce_scatter | solution.py:64
  195.3 5.0 copy-start.1
  374.4 2.8 copy-start.2
Sparse Core Ops, SparseCore 0:
  11.1 109.2 all-gather.2
  122.5 72.7 all-gather.4
  198.2 176.1 all-reduce.1
  379.3 146.3 reduce-scatter.1
where the time goes:
time: 533 us; the launch traced here: 532 us
  waiting for transfers between devices  496 us (93%)
  matrix products  16.1 us (3%)
  between operations  13.9 us (3%)
  other arithmetic  5.72 us (1%)
    psum x1, waiting for transfers between devices, finish_rows(): total = lax.psum(placed.astype(jnp.bfloat16), 'tensor').astype(jnp.float32)  170 us
    reduce_scatter x1, waiting for transfers between devices, body(): lax.psum_scatter(weight_term, 'dp', scatter_dimension=1, tiled=True)  147 us
    all_gather x1, waiting for transfers between devices, body(): full_weight = lax.all_gather(out_weight, 'dp', axis=1, tiled=True)  107 us
    all_gather x1, waiting for transfers between devices, body(): full_cot = lax.all_gather(cotangent, 'tensor', axis=1, tiled=True)  70.3 us
  transfers between devices with their start and end apart: 4, of which 4 were waited for; matrix products, arithmetic and copies ran while one was open for 4% of the time, Pallas kernels for 0%

commit v1 on v0

v1 whole, which is shorter than its diff:
```python
import functools
import math

import jax
import jax.numpy as jnp
from jax import lax
from jax.experimental import pallas as pl
from jax.experimental.pallas import tpu as pltpu
from jax.sharding import PartitionSpec as P

HD = 128
EPS = 1e-05
D_MODEL = 8192
MESH = pl.DeviceIdType.MESH
BF16 = jnp.bfloat16
F32 = jnp.float32
N_COPIES = 128


def kernel(
    queries,
    keys,
    values,
    starts_ref,
    weight,
    residual,
    gain,
    cot,
    mixed,
    normed,
    grad_weight,
    grad_heads,
    ho,
    ct,
    pp,
    p_tr,
    p_in,
    s_y,
    z_in,
    q_sum,
    t_in,
    gp,
    g_in,
    gs,
    gx_tr,
    gx_in,
    gh,
    gz_tr,
    gz_in,
    stream,
    sq,
    acc,
    ssem,
    rsem,
):
    dp, tensor = lax.axis_index("dp"), lax.axis_index("tensor")
    zh, x, c = dp // 8, (dp // 2) % 4, dp % 2
    zl, y = tensor // 4, tensor % 4

    def dev(zh_, x_, c_, zl_, y_):
        return ((zh_ * 4 + x_) * 2 + c_, zl_ * 4 + y_)

    def plus(a, k):
        return (a + k) % 4

    y_dev = {k: dev(zh, x, c, zl, plus(y, k)) for k in (1, 2, 3)}
    zl_dev = {k: dev(zh, x, c, plus(zl, k), y) for k in (1, 2, 3)}
    x_dev = {k: dev(zh, plus(x, k), c, zl, y) for k in (1, 3)}
    zh_dev = {k: dev(plus(zh, k), x, c, zl, y) for k in (1, 3)}
    sibling = dev(zh, x, 1 - c, zl, y)
    t_same, t_other = dev(zl, y, c, zh, x), dev(zl, y, 1 - c, zh, x)
    off_diagonal = (zh != zl) | (x != y)
    on_diagonal = (zh == zl) & (x == y)

    barrier = pltpu.get_barrier_semaphore()
    partners = [*y_dev.values(), *zl_dev.values(), *x_dev.values(), *zh_dev.values(), sibling]
    for partner in partners:
        pl.semaphore_signal(barrier, inc=1, device_id=partner, device_id_type=MESH)

    @pl.when(off_diagonal)
    def _():
        for partner in (t_same, t_other):
            pl.semaphore_signal(barrier, inc=1, device_id=partner, device_id_type=MESH)
        pl.semaphore_wait(barrier, len(partners) + 2)

    @pl.when(on_diagonal)
    def _():
        pl.semaphore_wait(barrier, len(partners))

    sent = []
    used = [0]

    def copy(src, dst, device):
        index = used[0]
        used[0] += 1
        return pltpu.make_async_remote_copy(
            src_ref=src,
            dst_ref=dst,
            send_sem=ssem.at[index],
            recv_sem=rsem.at[index],
            device_id=device,
            device_id_type=MESH,
        )

    def send(src, dst, device):
        made = copy(src, dst, device)
        made.start()
        sent.append(made)
        return made

    def transposed(own_src, other_src, dst):
        other = send(other_src, dst, t_other)
        same = copy(own_src, dst, t_same)

        @pl.when(off_diagonal)
        def _():
            same.start()

        @pl.when(on_diagonal)
        def _():
            dst[...] = own_src[...]

        def wait():
            other.wait_recv()

            @pl.when(off_diagonal)
            def _():
                same.wait()

        return wait

    class Gather:
        def __init__(self, slot, half, me, right, left):
            self.half, self.me, self.right, self.left = half, me, right, left
            self.to_right = send(slot(me), slot(me), right)
            self.to_left = send(slot(me), slot(me), left)

        def forward(self):
            self.to_right.wait_recv()
            half = self.half(plus(self.me, 3), 0)
            self.on_right = send(half, half, self.right)
            self.to_left.wait_recv()
            half = self.half(plus(self.me, 1), 1)
            self.on_left = send(half, half, self.left)

        def finish(self):
            self.on_right.wait_recv()
            self.on_left.wait_recv()

    class Reduce:
        def __init__(self, half, tr, arrived, me, right, left):
            self.half, self.tr, self.arrived, self.me = half, tr, arrived, me
            self.right, self.left = right, left
            opposite = plus(me, 2)
            self.t0 = send(half(opposite, 0), tr(0), right)
            self.t1 = send(half(opposite, 1), tr(1), left)
            self.r1 = send(half(plus(me, 1), 1), arrived(0, 1), right)
            self.l0 = send(half(plus(me, 3), 0), arrived(1, 0), left)

        def forward(self):
            self.t0.wait_recv()
            term = self.half(plus(self.me, 1), 0)
            term[...] = (term[...].astype(F32) + self.tr(0)[...].astype(F32)).astype(BF16)
            self.r0 = send(term, self.arrived(0, 0), self.right)
            self.t1.wait_recv()
            term = self.half(plus(self.me, 3), 1)
            term[...] = (term[...].astype(F32) + self.tr(1)[...].astype(F32)).astype(BF16)
            self.l1 = send(term, self.arrived(1, 1), self.left)

        def finish(self, h):
            (self.r0 if h == 0 else self.r1).wait_recv()
            (self.l0 if h == 0 else self.l1).wait_recv()
            return (
                self.half(self.me, h)[...].astype(F32)
                + self.arrived(0, h)[...].astype(F32)
                + self.arrived(1, h)[...].astype(F32)
            )

    def cot_half(k):
        return cot.at[:, pl.ds(pl.multiple_of(k * 256, 256), 256)]

    cot_wait = transposed(cot_half(c), cot_half(1 - c), ct.at[zh, x, c])

    kv = tensor // 2
    kv_cols = pl.ds(pl.multiple_of(kv * HD, HD), HD)
    key_rows, value_rows = keys[:, kv_cols], values[:, kv_cols]
    starts = jnp.broadcast_to(starts_ref[...] - dp * 128, (128, 128)).T
    row = lax.broadcasted_iota(jnp.int32, (128, 128), 0)
    col = lax.broadcasted_iota(jnp.int32, (128, 128), 1)
    allowed = (col >= starts) & (col <= row)
    for head in range(2):
        scores = lax.dot_general(
            queries[:, head * HD : (head + 1) * HD],
            key_rows,
            (((1,), (1,)), ((), ())),
            preferred_element_type=F32,
        ) / math.sqrt(HD)
        scores = jnp.where(allowed, scores, -1e30)
        top = jnp.max(scores, axis=-1, keepdims=True)
        weights = jnp.where(allowed, jnp.exp(scores - top), 0.0)
        probs = (weights / jnp.sum(weights, axis=-1, keepdims=True)).astype(BF16)
        ho[zh, x, c, :, head * HD : (head + 1) * HD] = jnp.dot(
            probs, value_rows, preferred_element_type=F32
        ).astype(BF16)

    def rows64(h):
        return pl.ds(h * 64, 64)

    def ho_x(g):
        return Gather(
            lambda o: ho.at[g, o, c],
            lambda o, h: ho.at[g, o, c, rows64(h)],
            x,
            x_dev[1],
            x_dev[3],
        )

    def ct_y(g):
        return Gather(
            lambda o: ct.at[g, o], lambda o, h: ct.at[g, o, h], y, y_dev[1], y_dev[3]
        )

    def ho_core(g):
        return send(ho.at[g, :, c], ho.at[g, :, c], sibling)

    ho_z = Gather(
        lambda o: ho.at[o, x, c],
        lambda o, h: ho.at[o, x, c, rows64(h)],
        zh,
        zh_dev[1],
        zh_dev[3],
    )
    groups = [zh, plus(zh, 3), plus(zh, 1), plus(zh, 2)]
    hx = [ho_x(groups[0])]

    cot_wait()
    ct_zl = [send(ct.at[zl, y], ct.at[zl, y], zl_dev[k]) for k in (1, 2, 3)]
    cgroups = [zl, plus(zl, 3), plus(zl, 2), plus(zl, 1)]
    cy = [ct_y(cgroups[0])]

    hx[0].forward()
    ho_z.forward()
    hx.append(ho_x(groups[1]))
    hx.append(ho_x(groups[2]))
    hx[0].finish()
    hc = [ho_core(groups[0])]
    for k in range(3):
        ct_zl[k].wait_recv()
        cy.append(ct_y(cgroups[k + 1]))
    cy[0].forward()

    def project(g):
        def tile(i, carry):
            rows = ho[g, i].reshape(256, 256)
            pp[g, i] = (
                jnp.dot(rows, weight[...], preferred_element_type=F32)
                .astype(BF16)
                .reshape(2, 128, 256)
            )
            return carry

        lax.fori_loop(0, 4, tile, 0)
        return Reduce(
            lambda o, h: pp.at[g, o, h],
            lambda h: p_tr.at[g, h],
            lambda side, h: p_in.at[g, side, h],
            y,
            y_dev[1],
            y_dev[3],
        )

    hc[0].wait_recv()
    py = [project(groups[0])]
    hx[1].forward()
    hx[2].forward()
    ho_z.finish()
    hx.append(ho_x(groups[3]))
    for k in (1, 2):
        hx[k].finish()
        hc.append(ho_core(groups[k]))
    for k in (1, 2, 3):
        cy[k].forward()
    py[0].forward()
    for k in (1, 2):
        hc[k].wait_recv()
        py.append(project(groups[k]))
    hx[3].forward()
    hx[3].finish()
    hc.append(ho_core(groups[3]))
    hc[3].wait_recv()
    py.append(project(groups[3]))

    def heads_grad(g):
        def tile(i, carry):
            rows = ct[g, i].reshape(256, 256)
            gp[g, i] = (
                lax.dot_general(
                    rows, weight[...], (((1,), (1,)), ((), ())), preferred_element_type=F32
                )
                .astype(BF16)
                .reshape(2, 128, 256)
            )
            return carry

        lax.fori_loop(0, 4, tile, 0)
        return send(gp.at[g, :, 1 - c], g_in.at[g], sibling)

    def heads_x(g, from_core):
        from_core.wait_recv()

        def tile(i, carry):
            gs[g, i] = (gp[g, i, c].astype(F32) + g_in[g, i].astype(F32)).astype(BF16)
            return carry

        lax.fori_loop(0, 4, tile, 0)
        return Reduce(
            lambda o, h: gs.at[g, o, rows64(h)],
            lambda h: gx_tr.at[g, h],
            lambda side, h: gx_in.at[g, side, rows64(h)],
            x,
            x_dev[1],
            x_dev[3],
        )

    gc = []
    for k in range(4):
        cy[k].finish()
        gc.append(heads_grad(cgroups[k]))
        if k >= 1:
            py[k].forward()
    gx = [heads_x(cgroups[k], gc[k]) for k in range(4)]

    for k in range(4):
        for h in range(2):
            s_y[groups[k], h] = py[k].finish(h).astype(BF16)
    pz = [send(s_y.at[plus(zl, k)], z_in.at[k - 1], zl_dev[k]) for k in (1, 2, 3)]

    for k in range(4):
        gx[k].forward()
    for k in range(4):
        for h in range(2):
            gh[cgroups[k], rows64(h)] = gx[k].finish(h).astype(BF16)
    gz = Reduce(
        lambda o, h: gh.at[o, rows64(h)],
        lambda h: gz_tr.at[h],
        lambda side, h: gz_in.at[side, rows64(h)],
        zh,
        zh_dev[1],
        zh_dev[3],
    )

    for k in range(3):
        pz[k].wait_recv()
    for h in range(2):
        q_sum[h] = (
            s_y[zl, h].astype(F32)
            + z_in[0, h].astype(F32)
            + z_in[1, h].astype(F32)
            + z_in[2, h].astype(F32)
        ).astype(BF16)
    p_wait = transposed(q_sum.at[c], q_sum.at[1 - c], t_in.at[c])

    acc[...] = jnp.zeros_like(acc)

    def weight_tile(i, carry):
        a, b = i // 4, i % 4
        acc[...] += lax.dot_general(
            ho[a, b].reshape(256, 256),
            ct[a, b].reshape(256, 256),
            (((0,), (0,)), ((), ())),
            preferred_element_type=F32,
        )
        return carry

    lax.fori_loop(0, 16, weight_tile, 0)
    grad_weight[...] = acc[...].astype(BF16)

    gz.forward()

    p_wait()
    squares = jnp.zeros((128, 1), F32)
    for k in range(2):
        cols = slice(k * 256, (k + 1) * 256)
        part = residual[:, cols].astype(F32) + t_in[k].astype(F32)
        stream[:, cols] = part
        mixed[:, cols] = part.astype(BF16)
        squares = squares + jnp.sum(part * part, axis=1, keepdims=True)
    sq[0] = jnp.broadcast_to(squares, (128, 128)).T[:8]
    nz = [send(sq.at[0], sq.at[k], zl_dev[k]) for k in (1, 2, 3)]
    for k in range(3):
        nz[k].wait_recv()
    sq[4] = sq[0] + sq[1] + sq[2] + sq[3]
    ny = [send(sq.at[4], sq.at[4 + k], y_dev[k]) for k in (1, 2, 3)]

    for h in range(2):
        grad_heads[h * 64 : (h + 1) * 64, :] = gz.finish(h).astype(BF16)

    for k in range(3):
        ny[k].wait_recv()
    total = sq[4] + sq[5] + sq[6] + sq[7]
    mean_square = jnp.broadcast_to(total[:1], (128, 128)).T[:, :1] / D_MODEL
    factor = lax.rsqrt(mean_square + EPS)
    normed[...] = (stream[...] * factor * gain[...].astype(F32)).astype(BF16)

    for made in sent:
        made.wait_send()


def body(queries, keys, values, doc_start, out_weight, residual, gain, cotangent):
    vmem = pl.BlockSpec(memory_space=pltpu.VMEM)

    def buf(*shape):
        return pltpu.VMEM(shape, BF16)

    return pl.pallas_call(
        kernel,
        out_shape=(
            jax.ShapeDtypeStruct((128, 512), BF16),
            jax.ShapeDtypeStruct((128, 512), BF16),
            jax.ShapeDtypeStruct((256, 256), BF16),
            jax.ShapeDtypeStruct((128, 256), BF16),
        ),
        in_specs=[vmem] * 8,
        out_specs=(vmem,) * 4,
        scratch_shapes=[
            buf(4, 4, 2, 128, 256),
            buf(4, 4, 2, 128, 256),
            buf(4, 4, 2, 128, 256),
            buf(4, 2, 128, 256),
            buf(4, 2, 2, 128, 256),
            buf(4, 2, 128, 256),
            buf(3, 2, 128, 256),
            buf(2, 128, 256),
            buf(2, 128, 256),
            buf(4, 4, 2, 128, 256),
            buf(4, 4, 128, 256),
            buf(4, 4, 128, 256),
            buf(4, 2, 64, 256),
            buf(4, 2, 128, 256),
            buf(4, 128, 256),
            buf(2, 64, 256),
            buf(2, 128, 256),
            pltpu.VMEM((128, 512), F32),
            pltpu.VMEM((8, 8, 128), F32),
            pltpu.VMEM((256, 256), F32),
            pltpu.SemaphoreType.DMA((N_COPIES,)),
            pltpu.SemaphoreType.DMA((N_COPIES,)),
        ],
        compiler_params=pltpu.CompilerParams(
            collective_id=0, has_side_effects=True, vmem_limit_bytes=32 * 2**20
        ),
    )(
        queries,
        keys,
        values,
        doc_start.reshape(1, 128),
        out_weight,
        residual,
        gain.reshape(1, 512),
        cotangent,
    )


def solution(mesh):
    placed = (
        P("dp", "tensor"),
        P("dp", None),
        P("dp", None),
        P("dp"),
        P("tensor", "dp"),
        P("dp", "tensor"),
        P("tensor"),
        P("dp", "tensor"),
    )
    return jax.shard_map(
        body,
        mesh=mesh,
        in_specs=placed,
        out_specs=(P("dp", "tensor"), P("dp", "tensor"), P("tensor", "dp"), P("dp", "tensor")),
        check_vma=False,
    )
```

time: 533 us -> 125 us (0.23)
  the two profiles are of different devices: /device:TPU:1 before, /device:TPU:482 now
where the time goes in v1:
time: 125 us
  Pallas kernels  115 us (92%)
  local copies, waits for them, and re-layouts  9.37 us (7%)
    pallas_call x1, Pallas kernels, body(): pl.pallas_call(kernel, out_shape=(jax.ShapeDtypeStruct((128, 512), BF16),...  115 us
    unnamed x20, local copies, waits for them, and re-layouts  9.37 us

profile of v1, /device:TPU:482, one launch (start us, length us, event | category | flops | bytes accessed | tf_op | source)
XLA Modules:
  0.0 124.9 jit_solution(1850262098023655806)
XLA Ops:
  0.6 0.0 copy-start.7
  0.6 0.7 copy-done.7
  1.3 0.0 copy-start.6
  1.3 0.6 copy-done.6
  2.0 0.0 copy-start
  2.0 0.9 copy-done
  2.9 0.0 copy-start.1
  2.9 0.9 copy-done.1
  3.9 0.0 copy-start.2
  3.9 0.9 copy-done.2
  4.8 0.0 copy-start.3
  4.8 0.9 copy-done.3
  5.7 0.0 copy-start.4
  5.7 0.9 copy-done.4
  6.6 0.0 copy-start.5
  6.6 0.8 copy-done.5
  7.4 114.9 %shard_map.111 = (bf16[128,512]{1,0:T(8,128)(2,1)S(1)}, bf16[128,512]{1,0:T(8,128)(2,1)S(1)}, bf16[256,256]{1,0:T(8,128)(2,1)S(1)}, bf16[128,256]{1,0:T(8,128)(2,1)S(1)}) custom-call(bf16[128,256]{1,0:T(8,128)(2,1)S(1)} %copy-done.5, bf16[128,1024]{1,0:T(8,128)(2,1)S(1)} %copy-done, bf16[128,1024]{1,0:T(8,128)(2,1)S(1)} %copy-done.1, s32[1,128]{1,0:T(1,128)S(1)} %bitcast.1, ...), custom_call_target="tpu_custom_call" | custom-call | tf_op jit(solution)/shard_map/pallas_call | solution.py:415
  122.3 0.7 copy.16
  122.9 0.7 copy.17
  123.6 0.7 copy.18
  124.3 0.6 copy.19
  (1 shorter events, 0.0 us)
Async XLA Ops:
  0.6 0.7 copy-start.7
  1.3 0.7 copy-start.6
  2.0 0.9 copy-start
  2.9 0.9 copy-start.1
  3.9 0.9 copy-start.2
  4.8 0.9 copy-start.3
  5.7 0.9 copy-start.4
  6.6 0.8 copy-start.5

commit v2 on v1

v2 whole, which is shorter than its diff:
```python
import functools
import math

import jax
import jax.numpy as jnp
from jax import lax
from jax.experimental import pallas as pl
from jax.experimental.pallas import tpu as pltpu
from jax.sharding import PartitionSpec as P

HD = 128
EPS = 1e-05
D_MODEL = 8192
MESH = pl.DeviceIdType.MESH
BF16 = jnp.bfloat16
F32 = jnp.float32
N_COPIES = 176
N_LOADS = 8


def kernel(
    queries_hbm,
    keys_hbm,
    values_hbm,
    starts_hbm,
    weight_hbm,
    residual_hbm,
    gain_hbm,
    cot_hbm,
    mixed,
    normed,
    grad_weight,
    grad_heads,
    mine,
    ho,
    ct,
    wt,
    s_y,
    z_in,
    q_sum,
    t_in,
    gw,
    gw_tr,
    gw_in,
    gp,
    g_in,
    gs,
    gx_tr,
    gx_in,
    gh,
    gz_tr,
    gz_in,
    g_sum,
    g_land,
    stream,
    sq,
    queries,
    keys,
    values,
    starts_ref,
    residual,
    gain,
    cot,
    ssem,
    rsem,
    lsem,
):
    dp, tensor = lax.axis_index("dp"), lax.axis_index("tensor")
    zh, x, c = dp // 8, (dp // 2) % 4, dp % 2
    zl, y = tensor // 4, tensor % 4

    def dev(zh_, x_, c_, zl_, y_):
        return ((zh_ * 4 + x_) * 2 + c_, zl_ * 4 + y_)

    def plus(a, k):
        return (a + k) % 4

    y_dev = {k: dev(zh, x, c, zl, plus(y, k)) for k in (1, 3)}
    zl_dev = {k: dev(zh, x, c, plus(zl, k), y) for k in (1, 2, 3)}
    row_dev = {k: (dp, (tensor + k) % 16) for k in range(1, 16)}
    x_dev = {k: dev(zh, plus(x, k), c, zl, y) for k in (1, 3)}
    zh_dev = {k: dev(plus(zh, k), x, c, zl, y) for k in (1, 3)}
    sibling = dev(zh, x, 1 - c, zl, y)
    t_same, t_other = dev(zl, y, c, zh, x), dev(zl, y, 1 - c, zh, x)
    off_diagonal = (zh != zl) | (x != y)
    on_diagonal = (zh == zl) & (x == y)
    xy_dev = dev(zh, y, c, zl, x)

    kv = tensor // 2
    kv_cols = pl.ds(pl.multiple_of(kv * HD, HD), HD)
    loads = [
        pltpu.make_async_copy(src, dst, lsem.at[index])
        for index, (src, dst) in enumerate(
            (
                (cot_hbm, cot),
                (queries_hbm, queries),
                (keys_hbm.at[:, kv_cols], keys),
                (values_hbm.at[:, kv_cols], values),
                (starts_hbm, starts_ref),
                (weight_hbm, wt.at[y]),
                (residual_hbm, residual),
                (gain_hbm, gain),
            )
        )
    ]
    for load in loads:
        load.start()

    barrier = pltpu.get_barrier_semaphore()
    partners = [*row_dev.values(), *x_dev.values(), *zh_dev.values(), sibling]
    for partner in partners:
        pl.semaphore_signal(barrier, inc=1, device_id=partner, device_id_type=MESH)

    @pl.when(off_diagonal)
    def _():
        for partner in (t_same, t_other):
            pl.semaphore_signal(barrier, inc=1, device_id=partner, device_id_type=MESH)

    @pl.when(x != y)
    def _():
        pl.semaphore_signal(barrier, inc=1, device_id=xy_dev, device_id_type=MESH)
        pl.semaphore_wait(barrier, len(partners) + 3)

    @pl.when((x == y) & (zh != zl))
    def _():
        pl.semaphore_wait(barrier, len(partners) + 2)

    @pl.when(on_diagonal)
    def _():
        pl.semaphore_wait(barrier, len(partners))

    for load in loads:
        load.wait()

    sent = []
    used = [0]

    def copy(src, dst, device):
        index = used[0]
        used[0] += 1
        return pltpu.make_async_remote_copy(
            src_ref=src,
            dst_ref=dst,
            send_sem=ssem.at[index],
            recv_sem=rsem.at[index],
            device_id=device,
            device_id_type=MESH,
        )

    def send(src, dst, device):
        made = copy(src, dst, device)
        made.start()
        sent.append(made)
        return made

    def transposed(own_src, other_src, dst):
        other = send(other_src, dst, t_other)
        same = copy(own_src, dst, t_same)

        @pl.when(off_diagonal)
        def _():
            same.start()

        @pl.when(on_diagonal)
        def _():
            dst[...] = own_src[...]

        def wait():
            other.wait_recv()

            @pl.when(off_diagonal)
            def _():
                same.wait()

        return wait

    def swapped(src, dst):
        made = copy(src, dst, xy_dev)

        @pl.when(x != y)
        def _():
            made.start()

        @pl.when(x == y)
        def _():
            dst[...] = src[...]

        def wait():
            @pl.when(x != y)
            def _():
                made.wait()

        return wait

    class Gather:
        def __init__(self, half, me, right, left):
            self.half, self.me, self.right, self.left = half, me, right, left
            self.right0 = send(half(me, 0), half(me, 0), right)
            self.left1 = send(half(me, 1), half(me, 1), left)
            self.right1 = send(half(me, 1), half(me, 1), right)
            self.left0 = send(half(me, 0), half(me, 0), left)

        def forward(self):
            self.right0.wait_recv()
            half = self.half(plus(self.me, 3), 0)
            self.on_right = send(half, half, self.right)
            self.left1.wait_recv()
            half = self.half(plus(self.me, 1), 1)
            self.on_left = send(half, half, self.left)

        def neighbours(self):
            self.right1.wait_recv()
            self.left0.wait_recv()

        def finish(self):
            self.on_right.wait_recv()
            self.on_left.wait_recv()

    class Reduce:
        def __init__(self, half, tr, arrived, me, right, left):
            self.half, self.tr, self.arrived, self.me = half, tr, arrived, me
            self.right, self.left = right, left
            opposite = plus(me, 2)
            self.t0 = send(half(opposite, 0), tr(0), right)
            self.t1 = send(half(opposite, 1), tr(1), left)
            self.r1 = send(half(plus(me, 1), 1), arrived(0, 1), right)
            self.l0 = send(half(plus(me, 3), 0), arrived(1, 0), left)

        def forward(self):
            self.t0.wait_recv()
            term = self.half(plus(self.me, 1), 0)
            term[...] = (term[...].astype(F32) + self.tr(0)[...].astype(F32)).astype(BF16)
            self.r0 = send(term, self.arrived(0, 0), self.right)
            self.t1.wait_recv()
            term = self.half(plus(self.me, 3), 1)
            term[...] = (term[...].astype(F32) + self.tr(1)[...].astype(F32)).astype(BF16)
            self.l1 = send(term, self.arrived(1, 1), self.left)

        def finish(self, h):
            (self.r0 if h == 0 else self.r1).wait_recv()
            (self.l0 if h == 0 else self.l1).wait_recv()
            return (
                self.half(self.me, h)[...].astype(F32)
                + self.arrived(0, h)[...].astype(F32)
                + self.arrived(1, h)[...].astype(F32)
            )

    def cot_half(k):
        return cot.at[:, pl.ds(pl.multiple_of(k * 256, 256), 256)]

    cot_wait = transposed(cot_half(c), cot_half(1 - c), ct.at[zh, c])
    w_y = Gather(lambda o, h: wt.at[o, pl.ds(h * 128, 128)], y, y_dev[1], y_dev[3])

    key_rows, value_rows = keys[...], values[...]
    starts = jnp.broadcast_to(starts_ref[...] - dp * 128, (128, 128)).T
    row = lax.broadcasted_iota(jnp.int32, (128, 128), 0)
    col = lax.broadcasted_iota(jnp.int32, (128, 128), 1)
    allowed = (col >= starts) & (col <= row)
    for head in range(2):
        scores = lax.dot_general(
            queries[:, head * HD : (head + 1) * HD],
            key_rows,
            (((1,), (1,)), ((), ())),
            preferred_element_type=F32,
        ) / math.sqrt(HD)
        scores = jnp.where(allowed, scores, -1e30)
        top = jnp.max(scores, axis=-1, keepdims=True)
        weights = jnp.where(allowed, jnp.exp(scores - top), 0.0)
        probs = (weights / jnp.sum(weights, axis=-1, keepdims=True)).astype(BF16)
        mine[:, head * HD : (head + 1) * HD] = jnp.dot(
            probs, value_rows, preferred_element_type=F32
        ).astype(BF16)

    def rows64(h):
        return pl.ds(h * 64, 64)

    def ho_x(g):
        return Gather(lambda o, h: ho.at[g, o, c, rows64(h)], x, x_dev[1], x_dev[3])

    def ho_core(g):
        return send(ho.at[g, :, c], ho.at[g, :, c], sibling)

    z_base = used[0]
    used[0] += 4

    def z_copy(k, src):
        return pltpu.make_async_remote_copy(
            src_ref=src,
            dst_ref=z_in.at[k],
            send_sem=ssem.at[z_base + k],
            recv_sem=rsem.at[z_base + k],
            device_id=dev(zh, x, c, plus(zl, k), y),
            device_id_type=MESH,
        )

    def project(g):
        part = jnp.dot(ho[g, 0].reshape(256, 256), wt[0], preferred_element_type=F32)
        for i in range(1, 4):
            part = part + jnp.dot(
                ho[g, i].reshape(256, 256), wt[i], preferred_element_type=F32
            )
        s_y[g] = part.astype(BF16).reshape(2, 128, 256)
        k = plus(g, 4 - zl)

        @pl.when(k != 0)
        def _():
            z_copy(k, s_y.at[g]).start()

    def heads_grad(g):
        def tile(i, carry):
            gp[g, i] = (
                lax.dot_general(
                    ct[g].reshape(256, 256),
                    wt[i],
                    (((1,), (1,)), ((), ())),
                    preferred_element_type=F32,
                )
                .astype(BF16)
                .reshape(2, 128, 256)
            )
            return carry

        lax.fori_loop(0, 4, tile, 0)
        return send(gp.at[g, :, 1 - c], g_in.at[g], sibling)

    def heads_x(g, from_core):
        from_core.wait_recv()

        def tile(i, carry):
            gs[g, i] = (gp[g, i, c].astype(F32) + g_in[g, i].astype(F32)).astype(BF16)
            return carry

        lax.fori_loop(0, 4, tile, 0)
        return Reduce(
            lambda o, h: gs.at[g, o, rows64(h)],
            lambda h: gx_tr.at[g, h],
            lambda side, h: gx_in.at[g, side, rows64(h)],
            x,
            x_dev[1],
            x_dev[3],
        )

    mine_wait = swapped(mine, ho.at[zh, y, c])
    w_y.forward()
    mine_wait()
    ho_z = Gather(lambda o, h: ho.at[o, x, c, rows64(h)], zh, zh_dev[1], zh_dev[3])
    groups = [zh, plus(zh, 3), plus(zh, 1), plus(zh, 2)]
    cgroups = [zl, plus(zl, 3), plus(zl, 2), plus(zl, 1)]
    hx = [ho_x(groups[0])]
    cot_wait()
    ct_zl = [send(ct.at[zl], ct.at[zl], zl_dev[k]) for k in (1, 2, 3)]
    hx[0].forward()
    w_y.neighbours()
    w_y.finish()
    gc = [heads_grad(cgroups[0])]
    hx[0].neighbours()
    hx[0].finish()
    hc = [ho_core(groups[0])]
    ho_z.forward()
    ho_z.neighbours()
    hx.append(ho_x(groups[1]))
    hx.append(ho_x(groups[2]))
    hc[0].wait_recv()
    project(groups[0])
    gx = [heads_x(cgroups[0], gc[0])]
    hx[1].forward()
    hx[2].forward()
    ho_z.finish()
    hx.append(ho_x(groups[3]))
    for k in (1, 2):
        hx[k].neighbours()
        hx[k].finish()
        hc.append(ho_core(groups[k]))
    hx[3].forward()
    for k in (1, 2):
        hc[k].wait_recv()
        project(groups[k])
    hx[3].neighbours()
    hx[3].finish()
    hc.append(ho_core(groups[3]))
    hc[3].wait_recv()
    project(groups[3])
    for k in (1, 2, 3):
        ct_zl[k - 1].wait_recv()
        gc.append(heads_grad(cgroups[k]))
    for k in (1, 2, 3):
        gx.append(heads_x(cgroups[k], gc[k]))
    for k in range(4):
        gx[k].forward()

    def weight_tile(i, carry):
        part = jnp.zeros((256, 256), F32)
        for g in range(4):
            part = part + lax.dot_general(
                ho[g, i].reshape(256, 256),
                ct[g].reshape(256, 256),
                (((0,), (0,)), ((), ())),
                preferred_element_type=F32,
            )
        gw[i] = part.astype(BF16)
        return carry

    lax.fori_loop(0, 4, weight_tile, 0)
    gw_y = Reduce(
        lambda o, h: gw.at[o, pl.ds(h * 128, 128)],
        lambda h: gw_tr.at[h],
        lambda side, h: gw_in.at[side, pl.ds(h * 128, 128)],
        y,
        y_dev[1],
        y_dev[3],
    )

    for k in range(4):
        for h in range(2):
            gh[cgroups[k], rows64(h)] = gx[k].finish(h).astype(BF16)
    gz = Reduce(
        lambda o, h: gh.at[o, rows64(h)],
        lambda h: gz_tr.at[h],
        lambda side, h: gz_in.at[side, rows64(h)],
        zh,
        zh_dev[1],
        zh_dev[3],
    )

    for k in (1, 2, 3):
        z_copy(k, s_y.at[0]).wait_recv()
    for h in range(2):
        q_sum[h] = (
            s_y[zl, h].astype(F32)
            + z_in[1, h].astype(F32)
            + z_in[2, h].astype(F32)
            + z_in[3, h].astype(F32)
        ).astype(BF16)
    p_wait = transposed(q_sum.at[c], q_sum.at[1 - c], t_in.at[c])

    gw_y.forward()
    gz.forward()
    for h in range(2):
        grad_weight[h * 128 : (h + 1) * 128, :] = gw_y.finish(h).astype(BF16)

    p_wait()
    squares = jnp.zeros((128, 1), F32)
    for k in range(2):
        cols = slice(k * 256, (k + 1) * 256)
        part = residual[:, cols].astype(F32) + t_in[k].astype(F32)
        stream[:, cols] = part
        mixed[:, cols] = part.astype(BF16)
        squares = squares + jnp.sum(part * part, axis=1, keepdims=True)
    sq[0] = jnp.broadcast_to(squares, (128, 128)).T[:8]
    norms = [send(sq.at[0], sq.at[k], row_dev[k]) for k in range(1, 16)]

    for h in range(2):
        g_sum[h * 64 : (h + 1) * 64, :] = gz.finish(h).astype(BF16)
    g_wait = swapped(g_sum, g_land)

    for made in norms:
        made.wait_recv()
    total = jnp.sum(sq[...], axis=0)
    mean_square = jnp.broadcast_to(total[:1], (128, 128)).T[:, :1] / D_MODEL
    factor = lax.rsqrt(mean_square + EPS)
    normed[...] = (stream[...] * factor * gain[...].astype(F32)).astype(BF16)

    g_wait()
    grad_heads[...] = g_land[...]

    for made in sent:
        made.wait_send()
    for k in (1, 2, 3):
        z_copy(k, s_y.at[0]).wait_send()


def body(queries, keys, values, doc_start, out_weight, residual, gain, cotangent):
    vmem = pl.BlockSpec(memory_space=pltpu.VMEM)

    def buf(*shape):
        return pltpu.VMEM(shape, BF16)

    return pl.pallas_call(
        kernel,
        out_shape=(
            jax.ShapeDtypeStruct((128, 512), BF16),
            jax.ShapeDtypeStruct((128, 512), BF16),
            jax.ShapeDtypeStruct((256, 256), BF16),
            jax.ShapeDtypeStruct((128, 256), BF16),
        ),
        in_specs=[pl.BlockSpec(memory_space=pltpu.HBM)] * 8,
        out_specs=(vmem,) * 4,
        scratch_shapes=[
            buf(128, 256),
            buf(4, 4, 2, 128, 256),
            buf(4, 2, 128, 256),
            buf(4, 256, 256),
            buf(4, 2, 128, 256),
            buf(4, 2, 128, 256),
            buf(2, 128, 256),
            buf(2, 128, 256),
            buf(4, 256, 256),
            buf(2, 128, 256),
            buf(2, 256, 256),
            buf(4, 4, 2, 128, 256),
            buf(4, 4, 128, 256),
            buf(4, 4, 128, 256),
            buf(4, 2, 64, 256),
            buf(4, 2, 128, 256),
            buf(4, 128, 256),
            buf(2, 64, 256),
            buf(2, 128, 256),
            buf(128, 256),
            buf(128, 256),
            pltpu.VMEM((128, 512), F32),
            pltpu.VMEM((16, 8, 128), F32),
            buf(128, 256),
            buf(128, 128),
            buf(128, 128),
            pltpu.VMEM((1, 128), jnp.int32),
            buf(128, 512),
            buf(1, 512),
            buf(128, 512),
            pltpu.SemaphoreType.DMA((N_COPIES,)),
            pltpu.SemaphoreType.DMA((N_COPIES,)),
            pltpu.SemaphoreType.DMA((N_LOADS,)),
        ],
        compiler_params=pltpu.CompilerParams(
            collective_id=0, has_side_effects=True, vmem_limit_bytes=32 * 2**20
        ),
    )(
        queries,
        keys,
        values,
        doc_start.reshape(1, 128),
        out_weight,
        residual,
        gain.reshape(1, 512),
        cotangent,
    )


def solution(mesh):
    placed = (
        P("dp", "tensor"),
        P("dp", None),
        P("dp", None),
        P("dp"),
        P("tensor", "dp"),
        P("dp", "tensor"),
        P("tensor"),
        P("dp", "tensor"),
    )
    return jax.shard_map(
        body,
        mesh=mesh,
        in_specs=placed,
        out_specs=(P("dp", "tensor"), P("dp", "tensor"), P("tensor", "dp"), P("dp", "tensor")),
        check_vma=False,
    )
```

time: 125 us -> 113 us (0.904)
  the two profiles are of different devices: /device:TPU:482 before, /device:TPU:2 now
where the time goes in v2:
time: 113 us; the launch traced here: 112 us
  Pallas kernels  102 us (90%)
  local copies, waits for them, and re-layouts  9.37 us (8%)
    pallas_call x1, Pallas kernels, body(): pl.pallas_call(kernel, out_shape=(jax.ShapeDtypeStruct((128, 512), BF16),...  102 us
    unnamed x20, local copies, waits for them, and re-layouts  9.37 us

profile of v2, /device:TPU:2, one launch (start us, length us, event | category | flops | bytes accessed | tf_op | source)
XLA Modules:
  0.0 112.2 jit_solution(15811974973675185930)
XLA Ops:
  0.6 0.0 copy-start.7
  0.6 0.7 copy-done.7
  1.3 0.0 copy-start.6
  1.3 0.6 copy-done.6
  2.0 0.0 copy-start
  2.0 0.9 copy-done
  2.9 0.0 copy-start.1
  2.9 0.9 copy-done.1
  3.9 0.0 copy-start.2
  3.9 0.9 copy-done.2
  4.8 0.0 copy-start.3
  4.8 0.9 copy-done.3
  5.7 0.0 copy-start.4
  5.7 0.9 copy-done.4
  6.6 0.0 copy-start.5
  6.6 0.8 copy-done.5
  7.4 102.2 %shard_map.111 = (bf16[128,512]{1,0:T(8,128)(2,1)S(1)}, bf16[128,512]{1,0:T(8,128)(2,1)S(1)}, bf16[256,256]{1,0:T(8,128)(2,1)S(1)}, bf16[128,256]{1,0:T(8,128)(2,1)S(1)}) custom-call(bf16[128,256]{1,0:T(8,128)(2,1)S(1)} %copy-done.5, bf16[128,1024]{1,0:T(8,128)(2,1)S(1)} %copy-done, bf16[128,1024]{1,0:T(8,128)(2,1)S(1)} %copy-done.1, s32[1,128]{1,0:T(1,128)S(1)} %bitcast.1, ...), custom_call_target="tpu_custom_call" | custom-call | tf_op jit(solution)/shard_map/pallas_call | solution.py:478
  109.6 0.7 copy.16
  110.3 0.7 copy.17
  111.0 0.7 copy.18
  111.6 0.6 copy.19
  (1 shorter events, 0.0 us)
Async XLA Ops:
  0.6 0.7 copy-start.7
  1.3 0.7 copy-start.6
  2.0 0.9 copy-start
  2.9 0.9 copy-start.1
  3.9 0.9 copy-start.2
  4.8 0.9 copy-start.3
  5.7 0.9 copy-start.4
  6.6 0.8 copy-start.5

commit v3 on v2

--- a/solution.py
+++ b/solution.py
@@ -50,8 +50,7 @@
     gh,
     gz_tr,
     gz_in,
-    g_sum,
-    g_land,
+    g_own,
     stream,
     sq,
     queries,
@@ -85,6 +84,7 @@
     off_diagonal = (zh != zl) | (x != y)
     on_diagonal = (zh == zl) & (x == y)
     xy_dev = dev(zh, y, c, zl, x)
+    xy_zh_dev = {k: dev(plus(zh, k), y, c, zl, x) for k in (1, 3)}
 
     kv = tensor // 2
     kv_cols = pl.ds(pl.multiple_of(kv * HD, HD), HD)
@@ -107,7 +107,13 @@
         load.start()
 
     barrier = pltpu.get_barrier_semaphore()
-    partners = [*row_dev.values(), *x_dev.values(), *zh_dev.values(), sibling]
+    partners = [
+        *row_dev.values(),
+        *x_dev.values(),
+        *zh_dev.values(),
+        *xy_zh_dev.values(),
+        sibling,
+    ]
     for partner in partners:
         pl.semaphore_signal(barrier, inc=1, device_id=partner, device_id_type=MESH)
 
@@ -193,12 +199,15 @@
         return wait
 
     class Gather:
-        def __init__(self, half, me, right, left):
+        def __init__(self, half, me, right, left, first=None):
             self.half, self.me, self.right, self.left = half, me, right, left
-            self.right0 = send(half(me, 0), half(me, 0), right)
-            self.left1 = send(half(me, 1), half(me, 1), left)
-            self.right1 = send(half(me, 1), half(me, 1), right)
-            self.left0 = send(half(me, 0), half(me, 0), left)
+            src = dst = functools.partial(half, me)
+            if first is not None:
+                src, dst, right, left = first
+            self.right0 = send(src(0), dst(0), right)
+            self.left1 = send(src(1), dst(1), left)
+            self.right1 = send(src(1), dst(1), right)
+            self.left0 = send(src(0), dst(0), left)
 
         def forward(self):
             self.right0.wait_recv()
@@ -217,14 +226,15 @@
             self.on_left.wait_recv()
 
     class Reduce:
-        def __init__(self, half, tr, arrived, me, right, left):
+        def __init__(self, half, tr, arrived, me, right, left, last=None):
             self.half, self.tr, self.arrived, self.me = half, tr, arrived, me
-            self.right, self.left = right, left
+            last_right, last_left = (right, left) if last is None else last
+            self.right, self.left = last_right, last_left
             opposite = plus(me, 2)
             self.t0 = send(half(opposite, 0), tr(0), right)
             self.t1 = send(half(opposite, 1), tr(1), left)
-            self.r1 = send(half(plus(me, 1), 1), arrived(0, 1), right)
-            self.l0 = send(half(plus(me, 3), 0), arrived(1, 0), left)
+            self.r1 = send(half(plus(me, 1), 1), arrived(0, 1), last_right)
+            self.l0 = send(half(plus(me, 3), 0), arrived(1, 0), last_left)
 
         def forward(self):
             self.t0.wait_recv()
@@ -236,11 +246,12 @@
             term[...] = (term[...].astype(F32) + self.tr(1)[...].astype(F32)).astype(BF16)
             self.l1 = send(term, self.arrived(1, 1), self.left)
 
-        def finish(self, h):
+        def finish(self, h, own=None):
+            own = self.half(self.me, h) if own is None else own
             (self.r0 if h == 0 else self.r1).wait_recv()
             (self.l0 if h == 0 else self.l1).wait_recv()
             return (
-                self.half(self.me, h)[...].astype(F32)
+                own[...].astype(F32)
                 + self.arrived(0, h)[...].astype(F32)
                 + self.arrived(1, h)[...].astype(F32)
             )
@@ -340,29 +351,40 @@
             x_dev[3],
         )
 
+    ho_z = Gather(
+        lambda o, h: ho.at[o, x, c, rows64(h)],
+        zh,
+        zh_dev[1],
+        zh_dev[3],
+        (
+            lambda h: mine.at[rows64(h)],
+            lambda h: ho.at[zh, y, c, rows64(h)],
+            xy_zh_dev[1],
+            xy_zh_dev[3],
+        ),
+    )
     mine_wait = swapped(mine, ho.at[zh, y, c])
+    groups = [zh, plus(zh, 3), plus(zh, 1), plus(zh, 2)]
+    cgroups = [zl, plus(zl, 3), plus(zl, 2), plus(zl, 1)]
     w_y.forward()
     mine_wait()
-    ho_z = Gather(lambda o, h: ho.at[o, x, c, rows64(h)], zh, zh_dev[1], zh_dev[3])
-    groups = [zh, plus(zh, 3), plus(zh, 1), plus(zh, 2)]
-    cgroups = [zl, plus(zl, 3), plus(zl, 2), plus(zl, 1)]
     hx = [ho_x(groups[0])]
+    ho_z.forward()
     cot_wait()
     ct_zl = [send(ct.at[zl], ct.at[zl], zl_dev[k]) for k in (1, 2, 3)]
     hx[0].forward()
     w_y.neighbours()
     w_y.finish()
     gc = [heads_grad(cgroups[0])]
+    ho_z.neighbours()
+    hx.append(ho_x(groups[1]))
+    hx.append(ho_x(groups[2]))
     hx[0].neighbours()
     hx[0].finish()
     hc = [ho_core(groups[0])]
-    ho_z.forward()
-    ho_z.neighbours()
-    hx.append(ho_x(groups[1]))
-    hx.append(ho_x(groups[2]))
+    gx = [heads_x(cgroups[0], gc[0])]
     hc[0].wait_recv()
     project(groups[0])
-    gx = [heads_x(cgroups[0], gc[0])]
     hx[1].forward()
     hx[2].forward()
     ho_z.finish()
@@ -371,22 +393,47 @@
         hx[k].neighbours()
         hx[k].finish()
         hc.append(ho_core(groups[k]))
+    for k in (1, 2, 3):
+        ct_zl[k - 1].wait_recv()
+        gc.append(heads_grad(cgroups[k]))
+        if k < 3:
+            hc[k].wait_recv()
+            project(groups[k])
     hx[3].forward()
-    for k in (1, 2):
-        hc[k].wait_recv()
-        project(groups[k])
+    for k in (1, 2, 3):
+        gx.append(heads_x(cgroups[k], gc[k]))
+    gx[0].forward()
     hx[3].neighbours()
     hx[3].finish()
     hc.append(ho_core(groups[3]))
     hc[3].wait_recv()
     project(groups[3])
     for k in (1, 2, 3):
-        ct_zl[k - 1].wait_recv()
-        gc.append(heads_grad(cgroups[k]))
+        gx[k].forward()
+    for k in range(4):
+        for h in range(2):
+            gh[cgroups[k], rows64(h)] = gx[k].finish(h).astype(BF16)
+    gz = Reduce(
+        lambda o, h: gh.at[o, rows64(h)],
+        lambda h: gz_tr.at[h],
+        lambda side, h: gz_in.at[side, rows64(h)],
+        zh,
+        zh_dev[1],
+        zh_dev[3],
+        (xy_zh_dev[1], xy_zh_dev[3]),
+    )
+    own_wait = swapped(gh.at[zh], g_own)
+
     for k in (1, 2, 3):
-        gx.append(heads_x(cgroups[k], gc[k]))
-    for k in range(4):
-        gx[k].forward()
+        z_copy(k, s_y.at[0]).wait_recv()
+    for h in range(2):
+        q_sum[h] = (
+            s_y[zl, h].astype(F32)
+            + z_in[1, h].astype(F32)
+            + z_in[2, h].astype(F32)
+            + z_in[3, h].astype(F32)
+        ).astype(BF16)
+    p_wait = transposed(q_sum.at[c], q_sum.at[1 - c], t_in.at[c])
 
     def weight_tile(i, carry):
         part = jnp.zeros((256, 256), F32)
@@ -409,34 +456,8 @@
         y_dev[1],
         y_dev[3],
     )
-
-    for k in range(4):
-        for h in range(2):
-            gh[cgroups[k], rows64(h)] = gx[k].finish(h).astype(BF16)
-    gz = Reduce(
-        lambda o, h: gh.at[o, rows64(h)],
-        lambda h: gz_tr.at[h],
-        lambda side, h: gz_in.at[side, rows64(h)],
-        zh,
-        zh_dev[1],
-        zh_dev[3],
-    )
-
-    for k in (1, 2, 3):
-        z_copy(k, s_y.at[0]).wait_recv()
-    for h in range(2):
-        q_sum[h] = (
-            s_y[zl, h].astype(F32)
-            + z_in[1, h].astype(F32)
-            + z_in[2, h].astype(F32)
-            + z_in[3, h].astype(F32)
-        ).astype(BF16)
-    p_wait = transposed(q_sum.at[c], q_sum.at[1 - c], t_in.at[c])
-
+    gz.forward()
     gw_y.forward()
-    gz.forward()
-    for h in range(2):
-        grad_weight[h * 128 : (h + 1) * 128, :] = gw_y.finish(h).astype(BF16)
 
     p_wait()
     squares = jnp.zeros((128, 1), F32)
@@ -450,18 +471,20 @@
     norms = [send(sq.at[0], sq.at[k], row_dev[k]) for k in range(1, 16)]
 
     for h in range(2):
-        g_sum[h * 64 : (h + 1) * 64, :] = gz.finish(h).astype(BF16)
-    g_wait = swapped(g_sum, g_land)
+        grad_weight[h * 128 : (h + 1) * 128, :] = gw_y.finish(h).astype(BF16)
+    own_wait()
+    for h in range(2):
+        rows = g_own.at[rows64(h)]
+        grad_heads[h * 64 : (h + 1) * 64, :] = gz.finish(h, rows).astype(BF16)
 
     for made in norms:
         made.wait_recv()
     total = jnp.sum(sq[...], axis=0)
     mean_square = jnp.broadcast_to(total[:1], (128, 128)).T[:, :1] / D_MODEL
     factor = lax.rsqrt(mean_square + EPS)
-    normed[...] = (stream[...] * factor * gain[...].astype(F32)).astype(BF16)
-
-    g_wait()
-    grad_heads[...] = g_land[...]
+    for k in range(4):
+        cols = slice(k * 128, (k + 1) * 128)
+        normed[:, cols] = (stream[:, cols] * factor * gain[k : k + 1, :].astype(F32)).astype(BF16)
 
     for made in sent:
         made.wait_send()
@@ -506,7 +529,6 @@
             buf(2, 64, 256),
             buf(2, 128, 256),
             buf(128, 256),
-            buf(128, 256),
             pltpu.VMEM((128, 512), F32),
             pltpu.VMEM((16, 8, 128), F32),
             buf(128, 256),
@@ -514,14 +536,14 @@
             buf(128, 128),
             pltpu.VMEM((1, 128), jnp.int32),
             buf(128, 512),
-            buf(1, 512),
+            buf(4, 128),
             buf(128, 512),
             pltpu.SemaphoreType.DMA((N_COPIES,)),
             pltpu.SemaphoreType.DMA((N_COPIES,)),
             pltpu.SemaphoreType.DMA((N_LOADS,)),
         ],
         compiler_params=pltpu.CompilerParams(
-            collective_id=0, has_side_effects=True, vmem_limit_bytes=32 * 2**20
+            collective_id=0, has_side_effects=True, vmem_limit_bytes=63 * 2**20
         ),
     )(
         queries,
@@ -530,7 +552,7 @@
         doc_start.reshape(1, 128),
         out_weight,
         residual,
-        gain.reshape(1, 512),
+        gain.reshape(4, 128),
         cotangent,
     )
 

time: 113 us -> 104 us (0.920)
  the two profiles are of different devices: /device:TPU:2 before, /device:TPU:128 now
where the time goes in v3:
time: 104 us; the launch traced here: 103 us
  Pallas kernels  98.6 us (95%)
  local copies, waits for them, and re-layouts  4.05 us (4%)
    pallas_call x1, Pallas kernels, body(): pl.pallas_call(kernel, out_shape=(jax.ShapeDtypeStruct((128, 512), BF16),...  98.6 us
    unnamed x10, local copies, waits for them, and re-layouts  4.05 us

profile of v3, /device:TPU:128, one launch (start us, length us, event | category | flops | bytes accessed | tf_op | source)
XLA Modules:
  0.0 103.3 jit_solution(1516226160495055066)
XLA Ops:
  0.6 98.6 %shard_map.111 = (bf16[128,512]{1,0:T(8,128)(2,1)}, bf16[128,512]{1,0:T(8,128)(2,1)}, bf16[256,256]{1,0:T(8,128)(2,1)}, bf16[128,256]{1,0:T(8,128)(2,1)}) custom-call(bf16[128,256]{1,0:T(8,128)(2,1)} %queries_hbm.1, bf16[128,1024]{1,0:T(8,128)(2,1)} %keys_hbm.1, bf16[128,1024]{1,0:T(8,128)(2,1)} %values_hbm.1, s32[1,128]{1,0:T(1,128)} %bitcast.3, ...), custom_call_target="tpu_custom_call" | custom-call | tf_op jit(solution)/shard_map/pallas_call | solution.py:501
  99.3 0.0 copy-start.1
  99.3 1.6 %copy.16 = bf16[128,512]{1,0:T(8,128)(2,1)} copy(bf16[128,512]{1,0:T(8,128)(2,1)} %get-tuple-element.8) | data formatting | bytes 262144
  100.9 0.0 copy-done.1
  100.9 0.0 copy-start
  100.9 0.7 copy.17
  101.5 0.3 copy-done
  101.8 0.0 copy-start.2
  101.8 0.7 copy.18
  102.5 0.2 copy-done.2
  102.7 0.6 copy.19
Async XLA Ops:
  99.3 1.6 %copy-start.1 = (bf16[128,512]{1,0:T(8,128)(2,1)S(1)}, bf16[128,512]{1,0:T(8,128)(2,1)}, u32[]{:S(2)}) copy-start(bf16[128,512]{1,0:T(8,128)(2,1)} %get-tuple-element.9) | copy-start | bytes 393220
  100.9 1.0 copy-start
  101.8 0.9 copy-start.2

commit v4 on v3

--- a/solution.py
+++ b/solution.py
@@ -259,7 +259,6 @@
     def cot_half(k):
         return cot.at[:, pl.ds(pl.multiple_of(k * 256, 256), 256)]
 
-    cot_wait = transposed(cot_half(c), cot_half(1 - c), ct.at[zh, c])
     w_y = Gather(lambda o, h: wt.at[o, pl.ds(h * 128, 128)], y, y_dev[1], y_dev[3])
 
     key_rows, value_rows = keys[...], values[...]
@@ -364,21 +363,22 @@
         ),
     )
     mine_wait = swapped(mine, ho.at[zh, y, c])
+    cot_wait = transposed(cot_half(c), cot_half(1 - c), ct.at[zh, c])
     groups = [zh, plus(zh, 3), plus(zh, 1), plus(zh, 2)]
     cgroups = [zl, plus(zl, 3), plus(zl, 2), plus(zl, 1)]
     w_y.forward()
     mine_wait()
     hx = [ho_x(groups[0])]
     ho_z.forward()
-    cot_wait()
-    ct_zl = [send(ct.at[zl], ct.at[zl], zl_dev[k]) for k in (1, 2, 3)]
     hx[0].forward()
     w_y.neighbours()
     w_y.finish()
-    gc = [heads_grad(cgroups[0])]
     ho_z.neighbours()
     hx.append(ho_x(groups[1]))
     hx.append(ho_x(groups[2]))
+    cot_wait()
+    ct_zl = [send(ct.at[zl], ct.at[zl], zl_dev[k]) for k in (1, 2, 3)]
+    gc = [heads_grad(cgroups[0])]
     hx[0].neighbours()
     hx[0].finish()
     hc = [ho_core(groups[0])]
@@ -492,20 +492,31 @@
         z_copy(k, s_y.at[0]).wait_send()
 
 
+def copy_results(*refs):
+    sources, results, held = refs[:4], refs[4:8], refs[8:12]
+    in_sem, out_sem = refs[12:]
+    loads = [pltpu.make_async_copy(sources[k], held[k], in_sem.at[k]) for k in range(4)]
+    stores = [pltpu.make_async_copy(held[k], results[k], out_sem.at[k]) for k in range(4)]
+    for load in loads:
+        load.start()
+    for load, store in zip(loads, stores):
+        load.wait()
+        store.start()
+    for store in stores:
+        store.wait()
+
+
 def body(queries, keys, values, doc_start, out_weight, residual, gain, cotangent):
     vmem = pl.BlockSpec(memory_space=pltpu.VMEM)
 
     def buf(*shape):
         return pltpu.VMEM(shape, BF16)
 
-    return pl.pallas_call(
+    sizes = ((128, 512), (128, 512), (256, 256), (128, 256))
+    shapes = tuple(jax.ShapeDtypeStruct(size, BF16) for size in sizes)
+    results = pl.pallas_call(
         kernel,
-        out_shape=(
-            jax.ShapeDtypeStruct((128, 512), BF16),
-            jax.ShapeDtypeStruct((128, 512), BF16),
-            jax.ShapeDtypeStruct((256, 256), BF16),
-            jax.ShapeDtypeStruct((128, 256), BF16),
-        ),
+        out_shape=shapes,
         in_specs=[pl.BlockSpec(memory_space=pltpu.HBM)] * 8,
         out_specs=(vmem,) * 4,
         scratch_shapes=[
@@ -555,6 +566,19 @@
         gain.reshape(4, 128),
         cotangent,
     )
+    hbm = pl.BlockSpec(memory_space=pltpu.HBM)
+    return pl.pallas_call(
+        copy_results,
+        out_shape=shapes,
+        in_specs=[hbm] * 4,
+        out_specs=(hbm,) * 4,
+        scratch_shapes=[
+            *(buf(*size) for size in sizes),
+            pltpu.SemaphoreType.DMA((4,)),
+            pltpu.SemaphoreType.DMA((4,)),
+        ],
+        compiler_params=pltpu.CompilerParams(vmem_limit_bytes=63 * 2**20),
+    )(*results)
 
 
 def solution(mesh):

time: 104 us -> 100 us (0.962)
  local copies, waits for them, and re-layouts: 4.05 us -> 0 us
    unnamed x10 -> x0, local copies, waits for them, and re-layouts: 4.05 us -> none
    pallas_call x1 -> x2, Pallas kernels: 98.6 us -> 99.4 us  [the longest x1 97.7 us: body(): pl.pallas_call(kernel, out_shape=shapes, in_specs=[pl.BlockSpec(memory_sp...]
where the time goes in v4:
time: 100 us
  Pallas kernels  99.4 us (99%)
    pallas_call x1, Pallas kernels, body(): pl.pallas_call(kernel, out_shape=shapes, in_specs=[pl.BlockSpec(memory_sp...  97.7 us

profile of v4, /device:TPU:128, one launch (start us, length us, event | category | flops | bytes accessed | tf_op | source)
XLA Modules:
  0.0 100.1 jit_solution(3145812479152652532)
XLA Ops:
  0.6 97.7 %shard_map.111 = (bf16[128,512]{1,0:T(8,128)(2,1)}, bf16[128,512]{1,0:T(8,128)(2,1)}, bf16[256,256]{1,0:T(8,128)(2,1)}, bf16[128,256]{1,0:T(8,128)(2,1)}) custom-call(bf16[128,256]{1,0:T(8,128)(2,1)} %queries_hbm.1, bf16[128,1024]{1,0:T(8,128)(2,1)} %keys_hbm.1, bf16[128,1024]{1,0:T(8,128)(2,1)} %values_hbm.1, s32[1,128]{1,0:T(1,128)} %bitcast.3, ...), custom_call_target="tpu_custom_call" | custom-call | tf_op jit(solution)/shard_map/pallas_call | solution.py:517
  98.3 1.8 %shard_map.112 = (bf16[128,512]{1,0:T(8,128)(2,1)}, bf16[128,512]{1,0:T(8,128)(2,1)}, bf16[256,256]{1,0:T(8,128)(2,1)}, bf16[128,256]{1,0:T(8,128)(2,1)}) custom-call(bf16[128,512]{1,0:T(8,128)(2,1)} %get-tuple-element.8.refs_0_, bf16[128,512]{1,0:T(8,128)(2,1)} %get-tuple-element.9.refs_1_, bf16[256,256]{1,0:T(8,128)(2,1)} %get-tuple-element.10.refs_2_, ...), custom_call_target="tpu_custom_call" | custom-call | tf_op jit(solution)/shard_map/pallas_call | solution.py:570

commit v5 on v4

--- a/solution.py
+++ b/solution.py
@@ -77,7 +77,7 @@
     y_dev = {k: dev(zh, x, c, zl, plus(y, k)) for k in (1, 3)}
     zl_dev = {k: dev(zh, x, c, plus(zl, k), y) for k in (1, 2, 3)}
     row_dev = {k: (dp, (tensor + k) % 16) for k in range(1, 16)}
-    x_dev = {k: dev(zh, plus(x, k), c, zl, y) for k in (1, 3)}
+    x_dev = {k: dev(zh, plus(x, k), c, zl, y) for k in (1, 2, 3)}
     zh_dev = {k: dev(plus(zh, k), x, c, zl, y) for k in (1, 3)}
     sibling = dev(zh, x, 1 - c, zl, y)
     t_same, t_other = dev(zl, y, c, zh, x), dev(zl, y, 1 - c, zh, x)
@@ -388,7 +388,8 @@
     hx[1].forward()
     hx[2].forward()
     ho_z.finish()
-    hx.append(ho_x(groups[3]))
+    last = ho.at[groups[3], x, c]
+    hx_last = [send(last, last, x_dev[k]) for k in (1, 3, 2)]
     for k in (1, 2):
         hx[k].neighbours()
         hx[k].finish()
@@ -399,12 +400,11 @@
         if k < 3:
             hc[k].wait_recv()
             project(groups[k])
-    hx[3].forward()
     for k in (1, 2, 3):
         gx.append(heads_x(cgroups[k], gc[k]))
     gx[0].forward()
-    hx[3].neighbours()
-    hx[3].finish()
+    for made in hx_last:
+        made.wait_recv()
     hc.append(ho_core(groups[3]))
     hc[3].wait_recv()
     project(groups[3])

time: 100 us -> 100 us (level)
  no operation moved by 1% of the time
where the time goes in v5:
time: 100 us
  Pallas kernels  99.4 us (99%)
    pallas_call x1, Pallas kernels, body(): pl.pallas_call(kernel, out_shape=shapes, in_specs=[pl.BlockSpec(memory_sp...  97.6 us

profile of v5, /device:TPU:128, one launch (start us, length us, event | category | flops | bytes accessed | tf_op | source)
XLA Modules:
  0.0 100.0 jit_solution(17689873664108649437)
XLA Ops:
  0.6 97.6 %shard_map.111 = (bf16[128,512]{1,0:T(8,128)(2,1)}, bf16[128,512]{1,0:T(8,128)(2,1)}, bf16[256,256]{1,0:T(8,128)(2,1)}, bf16[128,256]{1,0:T(8,128)(2,1)}) custom-call(bf16[128,256]{1,0:T(8,128)(2,1)} %queries_hbm.1, bf16[128,1024]{1,0:T(8,128)(2,1)} %keys_hbm.1, bf16[128,1024]{1,0:T(8,128)(2,1)} %values_hbm.1, s32[1,128]{1,0:T(1,128)} %bitcast.3, ...), custom_call_target="tpu_custom_call" | custom-call | tf_op jit(solution)/shard_map/pallas_call | solution.py:517
  98.3 1.8 %shard_map.112 = (bf16[128,512]{1,0:T(8,128)(2,1)}, bf16[128,512]{1,0:T(8,128)(2,1)}, bf16[256,256]{1,0:T(8,128)(2,1)}, bf16[128,256]{1,0:T(8,128)(2,1)}) custom-call(bf16[128,512]{1,0:T(8,128)(2,1)} %get-tuple-element.8.refs_0_, bf16[128,512]{1,0:T(8,128)(2,1)} %get-tuple-element.9.refs_1_, bf16[256,256]{1,0:T(8,128)(2,1)} %get-tuple-element.10.refs_2_, ...), custom_call_target="tpu_custom_call" | custom-call | tf_op jit(solution)/shard_map/pallas_call | solution.py:570

commit v6 on v5

--- a/solution.py
+++ b/solution.py
@@ -435,6 +435,8 @@
         ).astype(BF16)
     p_wait = transposed(q_sum.at[c], q_sum.at[1 - c], t_in.at[c])
 
+    gz.forward()
+
     def weight_tile(i, carry):
         part = jnp.zeros((256, 256), F32)
         for g in range(4):
@@ -456,7 +458,6 @@
         y_dev[1],
         y_dev[3],
     )
-    gz.forward()
     gw_y.forward()
 
     p_wait()

time: 100 us -> 100 us (level)
  no operation moved by 1% of the time
where the time goes in v6:
time: 100 us
  Pallas kernels  99.4 us (99%)
    pallas_call x1, Pallas kernels, body(): pl.pallas_call(kernel, out_shape=shapes, in_specs=[pl.BlockSpec(memory_sp...  97.6 us

profile of v6, /device:TPU:128, one launch (start us, length us, event | category | flops | bytes accessed | tf_op | source)
XLA Modules:
  0.0 100.0 jit_solution(13138874113310281280)
XLA Ops:
  0.6 97.6 %shard_map.111 = (bf16[128,512]{1,0:T(8,128)(2,1)}, bf16[128,512]{1,0:T(8,128)(2,1)}, bf16[256,256]{1,0:T(8,128)(2,1)}, bf16[128,256]{1,0:T(8,128)(2,1)}) custom-call(bf16[128,256]{1,0:T(8,128)(2,1)} %queries_hbm.1, bf16[128,1024]{1,0:T(8,128)(2,1)} %keys_hbm.1, bf16[128,1024]{1,0:T(8,128)(2,1)} %values_hbm.1, s32[1,128]{1,0:T(1,128)} %bitcast.3, ...), custom_call_target="tpu_custom_call" | custom-call | tf_op jit(solution)/shard_map/pallas_call | solution.py:518
  98.3 1.8 %shard_map.112 = (bf16[128,512]{1,0:T(8,128)(2,1)}, bf16[128,512]{1,0:T(8,128)(2,1)}, bf16[256,256]{1,0:T(8,128)(2,1)}, bf16[128,256]{1,0:T(8,128)(2,1)}) custom-call(bf16[128,512]{1,0:T(8,128)(2,1)} %get-tuple-element.8.refs_0_, bf16[128,512]{1,0:T(8,128)(2,1)} %get-tuple-element.9.refs_1_, bf16[256,256]{1,0:T(8,128)(2,1)} %get-tuple-element.10.refs_2_, ...), custom_call_target="tpu_custom_call" | custom-call | tf_op jit(solution)/shard_map/pallas_call | solution.py:571
